TPU v7x, 32 devices: a whole 2x2x4 slice. The times are simulated.
32 devices in a mesh: grp: 2 (over y), dp: 4 (over z), mod: 4 (over x, core).
Axes of the slice: x: 2, y: 2, z: 4, core: 2. Of those that a mesh axis runs over, the one named last changes fastest.
Arguments:
- queries: bfloat16 [32, 16, 4096], P('dp', 'mod'), may hold values from -0.119628906 to 0.119628906
- batch: int32 [32], P('dp'), may hold values from 0 to 1
- inv_out: float32 [2, 16, 64, 64], P(None, 'mod'), as said below
- inv_in: float32 [2, 16, 64, 64], P(None, 'mod'), as said below
- train_store: bfloat16 [1024, 16, 4096], P(('grp', 'dp'), 'mod'), parts along dimension 0, may hold values from -6 to 6
- row_scale: float32 [1024, 16], P(('grp', 'dp'), 'mod'), parts along dimension 0, may hold values from 0.2 to 2
Outputs:
- scores: float32 [32, 1024], P('mod', ('grp', 'dp')), parts along dimension 1
There are 2 independent parts, one for each index of `grp`. A program takes and returns all parts, laid end to end along the dimension named above; an argument that names none is the same for every part. Nothing has to cross between parts.
Inputs may be any that keep to these rules, and one draw needn't show every extreme that they name: `inv_out`: symmetric, each matrix of the form diagonal plus a smaller symmetric part. `inv_in`: symmetric, each matrix of the form diagonal plus a smaller symmetric part.
All inputs are finite; a program needn't handle non-finite values.
Results may differ from a plain program's by a relative error of at most 0.0029.
Values may be sent and summed in bfloat16 or wider, within the bound.
A program may use at most 64 MiB of HBM per device.

v0:
```python
import jax
import jax.numpy as jnp
from jax import lax
from jax.sharding import PartitionSpec as P


def precondition(rows, groups, inv_out, inv_in):
    count, local_mods, flat = rows.shape
    width_out = inv_out.shape[-1]
    width_in = inv_in.shape[-1]
    grad = rows.astype(jnp.float32).reshape(count, local_mods, width_out, width_in)
    second = (groups == 1)[:, None, None, None]
    pick_out = jnp.where(second, inv_out[1][None], inv_out[0][None])
    pick_in = jnp.where(second, inv_in[1][None], inv_in[0][None])
    left = jnp.einsum("qmij,qmjk->qmik", pick_out, grad, precision=lax.Precision.HIGHEST)
    both = jnp.einsum("qmik,qmkl->qmil", left, pick_in, precision=lax.Precision.HIGHEST)
    return both.reshape(count, local_mods, flat).astype(jnp.bfloat16)


def shards(queries, batch, inv_out, inv_in, train_store, row_scale):
    all_rows, all_groups = (
        lax.all_gather(queries, "dp", axis=0, tiled=True),
        lax.all_gather(batch, "dp", axis=0, tiled=True),
    )
    ready = precondition(all_rows, all_groups, inv_out, inv_in)
    weights = jnp.transpose(row_scale)
    total_rows = ready.shape[0]
    own_count = total_rows // lax.axis_size("mod")
    raw = jnp.einsum("qmk,tmk->mqt", ready, train_store, preferred_element_type=jnp.float32)
    totals = lax.psum(jnp.sum(raw * weights[:, None, :], axis=0), "mod")
    offset = lax.axis_index("mod") * own_count
    return lax.dynamic_slice_in_dim(totals, offset, own_count, 0)


def solution(mesh):
    in_specs = (
        P("dp", "mod", None),
        P("dp"),
        P(None, "mod", None, None),
        P(None, "mod", None, None),
        P(("grp", "dp"), "mod", None),
        P(("grp", "dp"), "mod"),
    )
    out_specs = P("mod", ("grp", "dp"))
    return jax.shard_map(shards, mesh=mesh, in_specs=in_specs, out_specs=out_specs, check_vma=False)
```

profile of v0, /device:TPU:0, one launch (start us, length us, event | category | flops | bytes accessed | tf_op | source)
XLA Modules:
  0.0 74.9 jit_solution(4619521599850979245)
XLA Ops:
  6.5 0.0 all-gather.2.cloned.1.call-start
  6.5 0.7 all-gather.2.cloned.1.call-update
  7.3 1.2 %dynamic-slice = u32[1]{0:T(128)} dynamic-slice(u32[32]{0:T(128)} %constant.16, u32[]{:T(128)S(6)} %add.6), dynamic_slice_sizes={1} | dynamic-slice | bytes 12
  9.2 0.9 %dynamic-update-slice = s32[32]{0:T(128)S(1)} dynamic-update-slice(s32[32]{0:T(128)S(1)} %broadcast.2, s32[8]{0:T(128)} %param.7, u32[]{:T(128)} %bitcast) | dynamic-update-slice | bytes 68
  10.0 9.9 %all-reduce = s32[32]{0:T(128)S(1)} all-reduce(s32[32]{0:T(128)S(1)} %dynamic-update-slice), channel_id=1, replica_groups=mesh['grp'=2,'dp'=4,'mod'=4] {'dp'}, use_global_device_ids=true, to_apply=%add | all-reduce | flops 32 | bytes 256
  19.9 1.0 %slice_bitcast_fusion.3 = (f32[4,64,64]{2,1,0:T(8,128)S(1)}, f32[4,64,64]{2,1,0:T(8,128)S(1)}) fusion(f32[2,4,64,64]{3,2,1,0:T(8,128)} %param.8), kind=kLoop, calls=%fused_computation.19 | loop fusion | bytes 262144 | tf_op jit(solution)/shard_map/jit(_where)/broadcast_in_dim | solution.py:13
  20.9 1.0 %slice_bitcast_fusion.1 = (f32[4,64,64]{2,1,0:T(8,128)S(1)}, f32[4,64,64]{2,1,0:T(8,128)S(1)}) fusion(f32[2,4,64,64]{3,2,1,0:T(8,128)} %param.9), kind=kLoop, calls=%fused_computation.17 | loop fusion | bytes 262144 | tf_op jit(solution)/shard_map/jit(_where)/broadcast_in_dim | solution.py:14
  21.9 17.7 %all-gather.2.cloned.1.call-done = bf16[32,4,4096]{2,1,0:T(4,128)(2,1)} async-done(((bf16[8,4,4096]{2,1,0:T(4,128)(2,1)}), bf16[32,4,4096]{2,1,0:T(4,128)(2,1)}) %all-gather.2.cloned.1.call-update) | async-done | bytes 1048592 | tf_op jit(solution)/shard_map/all_gather | solution.py:22
  39.6 3.3 %reshape.7 = bf16[32,4,64,64]{3,2,1,0:T(8,128)(2,1)S(1)} reshape(bf16[32,4,4096]{2,1,0:T(4,128)(2,1)} %all-gather.2.cloned.1.call-done) | data formatting | bytes 2097152 | tf_op jit(solution)/shard_map/reshape | solution.py:11
  42.9 2.7 %fusion.4 = f32[32,4,64,64]{3,2,1,0:T(8,128)S(1)} fusion(bf16[32,4,64,64]{3,2,1,0:T(8,128)(2,1)S(1)} %reshape.7, f32[4,64,64]{2,1,0:T(8,128)S(1)} %get-tuple-element.8, f32[4,64,64]{2,1,0:T(8,128)S(1)} %get-tuple-element.7, pred[32]{0:T(512)(128)(4,1)S(1)} %broadcast_compare_fusion), kind=kOutput, calls=%fused_computation.4 | convolution fusion | flops 403177472 | bytes 3276832 | tf_op jit(solution)/shard_map/qmij,qmjk->qmik/dot_general | solution.py:15
  45.6 0.0 copy-start
  45.6 4.7 %fusion.12 = bf16[32,4,64,64]{3,2,1,0:T(8,128)(2,1)S(1)} fusion(f32[32,4,64,64]{3,2,1,0:T(8,128)S(1)} %fusion.4, f32[4,64,64]{2,1,0:T(8,128)S(1)} %get-tuple-element.6, f32[4,64,64]{2,1,0:T(8,128)S(1)} %get-tuple-element.5, pred[32]{0:T(512)(128)(4,1)S(1)} %broadcast_compare_fusion), kind=kOutput, calls=%fused_computation.12 | convolution fusion | flops 403701760 | bytes 3276832 | tf_op jit(solution)/shard_map/qmik,qmkl->qmil/dot_general | solution.py:16
  50.3 1.4 %convert_element_type.8 = bf16[32,4,4096]{2,1,0:T(4,128)(2,1)S(1)} reshape(bf16[32,4,64,64]{3,2,1,0:T(8,128)(2,1)S(1)} %fusion.12) | data formatting | bytes 2097152 | tf_op jit(solution)/shard_map/convert_element_type | solution.py:17
  51.7 0.0 copy-done
  51.7 5.0 %fusion.18 = f32[32,128]{1,0:T(8,128)S(1)} fusion(bf16[128,4,4096]{2,1,0:T(4,128)(2,1)} %param.10, bf16[32,4,4096]{2,1,0:T(4,128)(2,1)S(1)} %convert_element_type.8, f32[4,128]{1,0:T(4,128)S(1)} %bitcast.14), kind=kOutput, calls=%fused_computation.14 | convolution fusion | flops 134246400 | bytes 5261312 | tf_op jit(solution)/shard_map/qmk,tmk->mqt/dot_general | solution.py:29
  56.7 10.7 %psum.7 = f32[32,128]{1,0:T(8,128)S(1)} all-reduce(f32[32,128]{1,0:T(8,128)S(1)} %fusion.18), channel_id=1, replica_groups=mesh['grp'=2,'dp'=4,'mod'=4] {'mod'}, use_global_device_ids=true, to_apply=%region_1.2 | all-reduce | flops 4096 | bytes 32768 | tf_op jit(solution)/shard_map/psum | solution.py:30
  67.5 0.6 constant_dynamic-slice_fusion
  (2 shorter events, 0.0 us)
Async XLA Ops:
  6.5 33.1 %all-gather.2.cloned.1.call-start = ((), (), s32[]{:S(2)}) async-start(), calls=%async_computation | async-start | bytes 1310720 | tf_op jit(solution)/shard_map/all_gather | solution.py:22
  45.6 6.1 %copy-start = (f32[128,4]{0,1:T(4,128)S(1)}, f32[128,4]{0,1:T(4,128)}, u32[]{:S(2)}) copy-start(f32[128,4]{0,1:T(4,128)} %param.11) | copy-start | bytes 6148
Sparse Core Ops, SparseCore 0:
  8.9 30.6 all-gather.1
where the time goes:
time: 75.2 us; the launch traced here: 74.9 us
  blocking collectives  20.6 us (27%)
  waiting for transfers between devices  18.4 us (24%)
  between operations  14.1 us (19%)
  matrix products  12.4 us (16%)
  local copies, waits for them, and re-layouts  9.37 us (12%)
    all_gather x1, waiting for transfers between devices, shards(): lax.all_gather(queries, 'dp', axis=0, tiled=True)  17.7 us
    psum x1, blocking collectives, shards(): totals = lax.psum(jnp.sum(raw * weights[:, None, :], axis=0), 'mod')  10.7 us
    unnamed x1, blocking collectives  9.89 us
    dot_general x1, matrix products, shards(): jnp.einsum('qmk,tmk->mqt', ready, train_store, preferred_element_type=jnp...  5.01 us
    dot_general x1, matrix products, precondition(): jnp.einsum('qmik,qmkl->qmil', left, pick_in, precision=lax.Precision.HIGH...  4.68 us
    reshape x1, local copies, waits for them, and re-layouts, precondition(): rows.astype(jnp.float32).reshape(count, local_mods, width_out, width_in)  3.29 us
    dot_general x1, matrix products, precondition(): jnp.einsum('qmij,qmjk->qmik', pick_out, grad, precision=lax.Precision.HIG...  2.7 us
    unnamed x5, local copies, waits for them, and re-layouts  2.11 us
  transfers between devices with their start and end apart: 1, of which 1 were waited for; matrix products, arithmetic and copies ran while one was open for 5% of the time, Pallas kernels for 0%

commit v1 on v0

v1 whole, which is shorter than its diff:
```python
import functools

import jax
import jax.numpy as jnp
from jax import lax
from jax.experimental import pallas as pl
from jax.experimental.pallas import tpu as pltpu
from jax.sharding import PartitionSpec as P

F32 = jnp.float32
BF16 = jnp.bfloat16
MESH = pl.DeviceIdType.MESH
LANES = 128


def pieces(values):
    high = values.astype(BF16)
    low = (values - high.astype(F32)).astype(BF16)
    return high, low


def mat(a, b):
    return jnp.dot(a, b, preferred_element_type=F32)


def mat_t(a, b):
    return lax.dot_general(a, b, (((1,), (1,)), ((), ())), preferred_element_type=F32)


def iota(shape, dim):
    return lax.broadcasted_iota(jnp.int32, shape, dim)


def ones_where(cond):
    return jnp.where(cond, 1.0, 0.0).astype(BF16)


def three(values):
    high = values.astype(BF16)
    rest = values - high.astype(F32)
    mid = rest.astype(BF16)
    low = (rest - mid.astype(F32)).astype(BF16)
    return high, mid, low


def kernel(sizes, q_ref, batch_ref, out_ref_in, in_ref_in, train_ref, scale_ref, res_ref,
           tcat, preb, right, left, scale_x, part, got,
           t_sem, z_send, z_recv, y_send, y_recv, m_send, m_recv):
    dp, nmod, own_q, mods, width, tiles, rows_t = sizes
    half_q = own_q // 2
    group = 16
    kts = group // mods
    cuts = tiles // kts
    rows = tiles * mods
    cols = own_q * group
    y, z, md = lax.axis_index("grp"), lax.axis_index("dp"), lax.axis_index("mod")
    other = 1 - y

    barrier = pltpu.get_barrier_semaphore()
    pl.semaphore_signal(barrier, inc=1, device_id={"grp": other}, device_id_type=MESH)
    for s in range(1, dp):
        pl.semaphore_signal(barrier, inc=1, device_id={"dp": lax.rem(z + s, dp)}, device_id_type=MESH)
    for s in range(1, nmod):
        pl.semaphore_signal(barrier, inc=1, device_id={"mod": lax.rem(md + s, nmod)}, device_id_type=MESH)

    def train_copy(g):
        return pltpu.make_async_copy(
            train_ref.at[:, pl.ds(group * g, group), :],
            tcat.at[:, :, pl.ds(LANES * g, LANES)],
            t_sem.at[g],
        )

    for g in range(cuts):
        train_copy(g).start()

    spread = ones_where(iota((width, 4 * width), 0) == iota((width, 4 * width), 1) % width)
    shape4 = (mods, 2, width, 4 * width)
    block = iota(shape4, 3) // width
    keep_r = (block % 2) == ((block // 2) ^ iota(shape4, 1))
    line = iota((2 * rows, mods * width), 0)
    line_half, line_in = line // rows, line % rows
    src = iota((2 * rows, mods * width), 1)
    pick_rows = ones_where((src // width == line_in % mods) & (src % width == 2 * (line_in // mods) + line_half))
    lcol = iota((width, 2 * rows), 1)
    col_half, col_in = lcol // rows, lcol % rows
    pick_cols = [
        ones_where(iota((width, 2 * rows), 0) == 2 * (col_in // mods) + (col_half ^ h)) for h in range(2)
    ]
    keep_l = iota((rows, 2 * rows), 0) % mods == iota((rows, 2 * rows), 1) % mods
    for b in range(2):
        for i, piece in enumerate(pieces(in_ref_in[b].reshape(mods * width, width))):
            wide = mat(piece, spread).reshape(mods, 1, width, 4 * width)
            wide = jnp.where(keep_r, jnp.broadcast_to(wide, shape4), 0.0)
            right[b, i] = wide.reshape(mods * 2 * width, 4 * width).astype(BF16)
        for i, piece in enumerate(pieces(out_ref_in[b].reshape(mods * width, width))):
            lines = mat(pick_rows, piece).astype(BF16)
            for h in range(2):
                full = mat(lines[h * rows:(h + 1) * rows], pick_cols[h])
                left[b, i, h * rows:(h + 1) * rows] = jnp.where(keep_l, full, 0.0).astype(BF16)

    def precondition(q, slot, at):
        b = batch_ref[q]
        x = q_ref[q]
        row_mod = iota((rows, LANES), 0) % mods
        zero = jnp.zeros_like(x)
        wide = jnp.concatenate([jnp.where(row_mod == m, x, zero) for m in range(mods)], axis=1)
        pair = mat(wide, right[b, 0]) + mat(wide, right[b, 1])
        stacked = jnp.concatenate([pair[:, :LANES], pair[:, LANES:]], axis=0)
        high, low = pieces(stacked)
        both = mat(left[b, 0], high) + (mat(left[b, 0], low) + mat(left[b, 1], high))
        lane = iota((rows, LANES), 1)
        pre = jnp.where(lane < width, both[:rows], both[rows:]).astype(BF16)
        for g in range(cuts):
            preb[z, slot, at, :, g * LANES:(g + 1) * LANES] = pre[g * group:(g + 1) * group]

    for i in range(half_q):
        precondition(y * half_q + i, y, i)

    def z_copy(origin, target):
        return pltpu.make_async_remote_copy(
            src_ref=preb.at[origin, y], dst_ref=preb.at[origin, y],
            send_sem=z_send.at[target], recv_sem=z_recv.at[origin],
            device_id={"dp": target}, device_id_type=MESH)

    def y_copy(origin, part_at):
        return pltpu.make_async_remote_copy(
            src_ref=preb.at[origin, part_at], dst_ref=preb.at[origin, part_at],
            send_sem=y_send.at[origin], recv_sem=y_recv.at[origin],
            device_id={"grp": other}, device_id_type=MESH)

    def m_copy(to, frm):
        return pltpu.make_async_remote_copy(
            src_ref=part.at[to], dst_ref=got.at[frm],
            send_sem=m_send.at[to], recv_sem=m_recv.at[frm],
            device_id={"mod": to}, device_id_type=MESH)

    pl.semaphore_wait(barrier, dp + nmod - 1)
    for s in range(1, dp):
        z_copy(z, lax.rem(z + s, dp)).start()

    for i in range(half_q):
        precondition(other * half_q + i, other, i)

    pick_mod = ones_where(iota((mods, cols), 0) == iota((mods, cols), 1) % mods)
    scale_x[...] = sum(
        lax.dot_general(p, pick_mod, (((0,), (0,)), ((), ())), preferred_element_type=F32)
        for p in three(scale_ref[...]))
    fold = ones_where(iota((own_q, cols), 1) // group == iota((own_q, cols), 0))

    for g in range(cuts):
        train_copy(g).wait()

    def score(origin):
        pre = preb[origin].reshape(cols, cuts * LANES)
        raw = mat_t(tcat[...].reshape(rows_t * group, cuts * LANES), pre).reshape(rows_t, group, cols)
        keep = iota((rows_t, group, cols), 1) == iota((rows_t, group, cols), 2) % group
        picked = jnp.sum(jnp.where(keep, raw, 0.0), axis=1) * scale_x[...]
        part[origin] = sum(mat_t(fold, p) for p in three(picked))

        @pl.when(origin != md)
        def _():
            m_copy(origin, md).start()

    score(z)

    for s in range(1, dp):
        origin = lax.rem(z + dp - s, dp)
        z_copy(origin, origin).wait_recv()
        y_copy(origin, y).start()

    def step(s, carry):
        origin = lax.rem(z + dp - s, dp)
        y_copy(origin, other).wait_recv()
        score(origin)
        return carry

    lax.fori_loop(1, dp, step, 0)

    total = part[md]
    for s in range(1, nmod):
        frm = lax.rem(md + s, nmod)
        m_copy(md, frm).wait_recv()
        total = total + got[frm]
    res_ref[...] = total

    for s in range(1, dp):
        at = lax.rem(z + s, dp)
        z_copy(z, at).wait_send()
        y_copy(at, y).wait_send()
    for s in range(1, nmod):
        m_copy(lax.rem(md + s, nmod), md).wait_send()


def shards(queries, batch, inv_out, inv_in, train_store, row_scale):
    own_q, mods, flat = queries.shape
    width = inv_in.shape[-1]
    rows_t = train_store.shape[0]
    dp, nmod = lax.axis_size("dp"), lax.axis_size("mod")
    tiles = flat // LANES
    rows = tiles * mods

    def by_tile(a):
        return jnp.transpose(a.reshape(-1, mods, tiles, LANES), (0, 2, 1, 3)).reshape(-1, rows, LANES)

    sizes = (dp, nmod, own_q, mods, width, tiles, rows_t)
    vmem = pl.BlockSpec(memory_space=pltpu.VMEM)
    cuts = rows // 16
    return pl.pallas_call(
        functools.partial(kernel, sizes),
        out_shape=jax.ShapeDtypeStruct((own_q, rows_t), F32),
        in_specs=[vmem, pl.BlockSpec(memory_space=pltpu.SMEM), vmem, vmem,
                  pl.BlockSpec(memory_space=pl.ANY), vmem],
        out_specs=vmem,
        scratch_shapes=[
            pltpu.VMEM((rows_t, 16, cuts * LANES), BF16),
            pltpu.VMEM((dp, 2, own_q // 2, 16, cuts * LANES), BF16),
            pltpu.VMEM((2, 2, mods * 2 * width, 4 * width), BF16),
            pltpu.VMEM((2, 2, 2 * rows, 2 * rows), BF16),
            pltpu.VMEM((rows_t, own_q * 16), F32),
            pltpu.VMEM((nmod, own_q, rows_t), F32),
            pltpu.VMEM((nmod, own_q, rows_t), F32),
            pltpu.SemaphoreType.DMA((cuts,)),
            pltpu.SemaphoreType.DMA((dp,)),
            pltpu.SemaphoreType.DMA((dp,)),
            pltpu.SemaphoreType.DMA((dp,)),
            pltpu.SemaphoreType.DMA((dp,)),
            pltpu.SemaphoreType.DMA((nmod,)),
            pltpu.SemaphoreType.DMA((nmod,)),
        ],
        compiler_params=pltpu.CompilerParams(
            collective_id=0, has_side_effects=True, vmem_limit_bytes=40 * 1024 * 1024),
    )(by_tile(queries), batch, inv_out, inv_in, by_tile(train_store), jnp.transpose(row_scale))


def solution(mesh):
    in_specs = (
        P("dp", "mod", None),
        P("dp"),
        P(None, "mod", None, None),
        P(None, "mod", None, None),
        P(("grp", "dp"), "mod", None),
        P(("grp", "dp"), "mod"),
    )
    out_specs = P("mod", ("grp", "dp"))
    return jax.shard_map(shards, mesh=mesh, in_specs=in_specs, out_specs=out_specs, check_vma=False)
```

time: 75.2 us -> 36.2 us (0.48)
  the two profiles are of different devices: /device:TPU:0 before, /device:TPU:1 now
where the time goes in v1:
time: 36.2 us; the launch traced here: 35.9 us
  Pallas kernels  28.9 us (80%)
  local copies, waits for them, and re-layouts  6.97 us (19%)
    pallas_call x1, Pallas kernels, shards(): pl.pallas_call(functools.partial(kernel, sizes), out_shape=jax.ShapeDtype...  28.9 us
    unnamed x13, local copies, waits for them, and re-layouts  6.97 us

profile of v1, /device:TPU:1, one launch (start us, length us, event | category | flops | bytes accessed | tf_op | source)
XLA Modules:
  0.0 35.9 jit_solution(10841120197989164711)
XLA Ops:
  0.0 0.0 copy-start
  0.0 2.2 %copy-done = bf16[128,4,4096]{2,1,0:T(4,128)(2,1)S(1)} copy-done((bf16[128,4,4096]{2,1,0:T(4,128)(2,1)S(1)}, bf16[128,4,4096]{2,1,0:T(4,128)(2,1)}, u32[]{:S(2)}) %copy-start) | copy-done | bytes 4194328
  2.2 0.0 copy-start.1
  2.2 0.9 %copy-done.1 = bf16[8,4,4096]{2,1,0:T(4,128)(2,1)S(1)} copy-done((bf16[8,4,4096]{2,1,0:T(4,128)(2,1)S(1)}, bf16[8,4,4096]{2,1,0:T(4,128)(2,1)}, u32[]{:S(2)}) %copy-start.1) | copy-done | bytes 262168
  3.1 0.0 copy-start.2
  3.1 0.9 %copy-done.2 = f32[2,4,64,64]{3,2,1,0:T(8,128)S(1)} copy-done((f32[2,4,64,64]{3,2,1,0:T(8,128)S(1)}, f32[2,4,64,64]{3,2,1,0:T(8,128)}, u32[]{:S(2)}) %copy-start.2) | copy-done | bytes 131096
  4.1 0.0 copy-start.3
  4.1 0.9 %copy-done.3 = f32[2,4,64,64]{3,2,1,0:T(8,128)S(1)} copy-done((f32[2,4,64,64]{3,2,1,0:T(8,128)S(1)}, f32[2,4,64,64]{3,2,1,0:T(8,128)}, u32[]{:S(2)}) %copy-start.3) | copy-done | bytes 131096
  5.0 0.0 copy-start.4
  5.0 0.7 %copy-done.4 = f32[128,4]{0,1:T(4,128)S(1)} copy-done((f32[128,4]{0,1:T(4,128)S(1)}, f32[128,4]{0,1:T(4,128)}, u32[]{:S(2)}) %copy-start.4) | copy-done | bytes 2072
  5.7 0.0 copy-start.5
  5.7 0.7 %copy-done.5 = s32[8]{0:T(128)S(1)} copy-done((s32[8]{0:T(128)S(1)}, s32[8]{0:T(128)}, u32[]{:S(2)}) %copy-start.5) | copy-done | bytes 56
  6.4 28.9 %shard_map.64 = f32[8,128]{1,0:T(8,128)S(1)} custom-call(bf16[8,128,128]{2,1,0:T(8,128)(2,1)S(1)} %bitcast.12, s32[8]{0:T(128)S(1)} %copy-done.5, f32[2,4,64,64]{3,2,1,0:T(8,128)S(1)} %copy-done.2, f32[2,4,64,64]{3,2,1,0:T(8,128)S(1)} %copy-done.3, bf16[128,128,128]{2,1,0:T(8,128)(2,1)S(1)} %bitcast.11, f32[4,128]{1,0:T(4,128)S(1)} %bitcast.13), custom_call_target="tpu_custom_call" | custom-call | tf_op jit(solution)/shard_map/pallas_call | solution.py:208
  35.3 0.6 %copy.10 = f32[8,128]{1,0:T(8,128)} copy(f32[8,128]{1,0:T(8,128)S(1)} %shard_map.64) | data formatting | bytes 8192
Async XLA Ops:
  0.0 2.2 %copy-start = (bf16[128,4,4096]{2,1,0:T(4,128)(2,1)S(1)}, bf16[128,4,4096]{2,1,0:T(4,128)(2,1)}, u32[]{:S(2)}) copy-start(bf16[128,4,4096]{2,1,0:T(4,128)(2,1)} %param.10) | copy-start | bytes 12582916
  2.2 0.9 %copy-start.1 = (bf16[8,4,4096]{2,1,0:T(4,128)(2,1)S(1)}, bf16[8,4,4096]{2,1,0:T(4,128)(2,1)}, u32[]{:S(2)}) copy-start(bf16[8,4,4096]{2,1,0:T(4,128)(2,1)} %param.6) | copy-start | bytes 786436
  3.1 0.9 %copy-start.2 = (f32[2,4,64,64]{3,2,1,0:T(8,128)S(1)}, f32[2,4,64,64]{3,2,1,0:T(8,128)}, u32[]{:S(2)}) copy-start(f32[2,4,64,64]{3,2,1,0:T(8,128)} %out_ref_in.1) | copy-start | bytes 393220
  4.1 0.9 %copy-start.3 = (f32[2,4,64,64]{3,2,1,0:T(8,128)S(1)}, f32[2,4,64,64]{3,2,1,0:T(8,128)}, u32[]{:S(2)}) copy-start(f32[2,4,64,64]{3,2,1,0:T(8,128)} %in_ref_in.1) | copy-start | bytes 393220
  5.0 0.7 %copy-start.4 = (f32[128,4]{0,1:T(4,128)S(1)}, f32[128,4]{0,1:T(4,128)}, u32[]{:S(2)}) copy-start(f32[128,4]{0,1:T(4,128)} %param.11) | copy-start | bytes 6148
  5.7 0.7 %copy-start.5 = (s32[8]{0:T(128)S(1)}, s32[8]{0:T(128)}, u32[]{:S(2)}) copy-start(s32[8]{0:T(128)} %batch_ref.1) | copy-start | bytes 100

commit v2 on v1

--- a/solution.py
+++ b/solution.py
@@ -43,9 +43,10 @@
     return high, mid, low
 
 
-def kernel(sizes, q_ref, batch_ref, out_ref_in, in_ref_in, train_ref, scale_ref, res_ref,
+def kernel(sizes, q_hbm, batch_ref, out_hbm, in_hbm, train_ref, scale_hbm, res_ref,
+           q_ref, out_ref_in, in_ref_in, scale_ref,
            tcat, preb, right, left, scale_x, part, got,
-           t_sem, z_send, z_recv, y_send, y_recv, m_send, m_recv):
+           l_sem, t_sem, z_send, z_recv, y_send, y_recv, m_send, m_recv):
     dp, nmod, own_q, mods, width, tiles, rows_t = sizes
     half_q = own_q // 2
     group = 16
@@ -56,10 +57,25 @@
     y, z, md = lax.axis_index("grp"), lax.axis_index("dp"), lax.axis_index("mod")
     other = 1 - y
 
+    locals_in = [
+        pltpu.make_async_copy(src, dst, l_sem.at[i])
+        for i, (src, dst) in enumerate(
+            ((out_hbm, out_ref_in), (in_hbm, in_ref_in), (q_hbm, q_ref), (scale_hbm, scale_ref)))
+    ]
+    for copy in locals_in:
+        copy.start()
+
     barrier = pltpu.get_barrier_semaphore()
     pl.semaphore_signal(barrier, inc=1, device_id={"grp": other}, device_id_type=MESH)
-    for s in range(1, dp):
-        pl.semaphore_signal(barrier, inc=1, device_id={"dp": lax.rem(z + s, dp)}, device_id_type=MESH)
+
+    @pl.when(z > 0)
+    def _():
+        pl.semaphore_signal(barrier, inc=1, device_id={"dp": z - 1}, device_id_type=MESH)
+
+    @pl.when(z < dp - 1)
+    def _():
+        pl.semaphore_signal(barrier, inc=1, device_id={"dp": z + 1}, device_id_type=MESH)
+
     for s in range(1, nmod):
         pl.semaphore_signal(barrier, inc=1, device_id={"mod": lax.rem(md + s, nmod)}, device_id_type=MESH)
 
@@ -87,6 +103,8 @@
         ones_where(iota((width, 2 * rows), 0) == 2 * (col_in // mods) + (col_half ^ h)) for h in range(2)
     ]
     keep_l = iota((rows, 2 * rows), 0) % mods == iota((rows, 2 * rows), 1) % mods
+    locals_in[0].wait()
+    locals_in[1].wait()
     for b in range(2):
         for i, piece in enumerate(pieces(in_ref_in[b].reshape(mods * width, width))):
             wide = mat(piece, spread).reshape(mods, 1, width, 4 * width)
@@ -113,19 +131,16 @@
         for g in range(cuts):
             preb[z, slot, at, :, g * LANES:(g + 1) * LANES] = pre[g * group:(g + 1) * group]
 
-    for i in range(half_q):
-        precondition(y * half_q + i, y, i)
-
-    def z_copy(origin, target):
+    def z_copy(origin, i, way):
         return pltpu.make_async_remote_copy(
-            src_ref=preb.at[origin, y], dst_ref=preb.at[origin, y],
-            send_sem=z_send.at[target], recv_sem=z_recv.at[origin],
-            device_id={"dp": target}, device_id_type=MESH)
-
-    def y_copy(origin, part_at):
+            src_ref=preb.at[origin, y, i], dst_ref=preb.at[origin, y, i],
+            send_sem=z_send.at[way, origin, i], recv_sem=z_recv.at[origin, i],
+            device_id={"dp": z + (1 - 2 * way)}, device_id_type=MESH)
+
+    def y_copy(origin, part_at, i):
         return pltpu.make_async_remote_copy(
-            src_ref=preb.at[origin, part_at], dst_ref=preb.at[origin, part_at],
-            send_sem=y_send.at[origin], recv_sem=y_recv.at[origin],
+            src_ref=preb.at[origin, part_at, i], dst_ref=preb.at[origin, part_at, i],
+            send_sem=y_send.at[origin, i], recv_sem=y_recv.at[origin, i],
             device_id={"grp": other}, device_id_type=MESH)
 
     def m_copy(to, frm):
@@ -134,13 +149,29 @@
             send_sem=m_send.at[to], recv_sem=m_recv.at[frm],
             device_id={"mod": to}, device_id_type=MESH)
 
-    pl.semaphore_wait(barrier, dp + nmod - 1)
-    for s in range(1, dp):
-        z_copy(z, lax.rem(z + s, dp)).start()
-
+    def has_next(way):
+        return z < dp - 1 if way == 0 else z > 0
+
+    locals_in[2].wait()
     for i in range(half_q):
-        precondition(other * half_q + i, other, i)
-
+        precondition(y * half_q + i, y, i)
+        if i == 0:
+            at_end = (z == 0) | (z == dp - 1)
+
+            @pl.when(at_end)
+            def _():
+                pl.semaphore_wait(barrier, nmod + 1)
+
+            @pl.when(jnp.logical_not(at_end))
+            def _():
+                pl.semaphore_wait(barrier, nmod + 2)
+
+        for way in range(2):
+            @pl.when(has_next(way))
+            def _():
+                z_copy(z, i, way).start()
+
+    locals_in[3].wait()
     pick_mod = ones_where(iota((mods, cols), 0) == iota((mods, cols), 1) % mods)
     scale_x[...] = sum(
         lax.dot_general(p, pick_mod, (((0,), (0,)), ((), ())), preferred_element_type=F32)
@@ -161,20 +192,47 @@
         def _():
             m_copy(origin, md).start()
 
+    def source(d, way):
+        origin = z - d if way == 0 else z + d
+        return jnp.clip(origin, 0, dp - 1), (origin >= 0) & (origin < dp)
+
+    def pass_on(d, i):
+        for way in range(2):
+            origin, there = source(d, way)
+
+            @pl.when(there)
+            def _():
+                z_copy(origin, i, way).wait_recv()
+
+                @pl.when(has_next(way))
+                def _():
+                    z_copy(origin, i, way).start()
+
+                y_copy(origin, y, i).start()
+
+    def use(d):
+        for way in range(2):
+            origin, there = source(d, way)
+
+            @pl.when(there)
+            def _():
+                for i in range(half_q):
+                    y_copy(origin, other, i).wait_recv()
+                score(origin)
+
+    for i in range(half_q):
+        pass_on(1, i)
+        precondition(other * half_q + i, other, i)
     score(z)
 
-    for s in range(1, dp):
-        origin = lax.rem(z + dp - s, dp)
-        z_copy(origin, origin).wait_recv()
-        y_copy(origin, y).start()
-
-    def step(s, carry):
-        origin = lax.rem(z + dp - s, dp)
-        y_copy(origin, other).wait_recv()
-        score(origin)
+    def step(d, carry):
+        for i in range(half_q):
+            pass_on(d, i)
+        use(d - 1)
         return carry
 
-    lax.fori_loop(1, dp, step, 0)
+    lax.fori_loop(2, dp, step, 0)
+    use(dp - 1)
 
     total = part[md]
     for s in range(1, nmod):
@@ -183,10 +241,23 @@
         total = total + got[frm]
     res_ref[...] = total
 
-    for s in range(1, dp):
-        at = lax.rem(z + s, dp)
-        z_copy(z, at).wait_send()
-        y_copy(at, y).wait_send()
+    def drain(origin, carry):
+        for i in range(half_q):
+            @pl.when((origin <= z) & (z < dp - 1))
+            def _():
+                z_copy(origin, i, 0).wait_send()
+
+            @pl.when((origin >= z) & (z > 0))
+            def _():
+                z_copy(origin, i, 1).wait_send()
+
+            @pl.when(origin != z)
+            def _():
+                y_copy(origin, y, i).wait_send()
+
+        return carry
+
+    lax.fori_loop(0, dp, drain, 0)
     for s in range(1, nmod):
         m_copy(lax.rem(md + s, nmod), md).wait_send()
 
@@ -204,14 +275,19 @@
 
     sizes = (dp, nmod, own_q, mods, width, tiles, rows_t)
     vmem = pl.BlockSpec(memory_space=pltpu.VMEM)
+    hbm = pl.BlockSpec(memory_space=pl.ANY)
+    half_q = own_q // 2
     cuts = rows // 16
     return pl.pallas_call(
         functools.partial(kernel, sizes),
         out_shape=jax.ShapeDtypeStruct((own_q, rows_t), F32),
-        in_specs=[vmem, pl.BlockSpec(memory_space=pltpu.SMEM), vmem, vmem,
-                  pl.BlockSpec(memory_space=pl.ANY), vmem],
+        in_specs=[hbm, pl.BlockSpec(memory_space=pltpu.SMEM), hbm, hbm, hbm, hbm],
         out_specs=vmem,
         scratch_shapes=[
+            pltpu.VMEM((own_q, rows, LANES), BF16),
+            pltpu.VMEM(inv_out.shape, F32),
+            pltpu.VMEM(inv_in.shape, F32),
+            pltpu.VMEM((mods, rows_t), F32),
             pltpu.VMEM((rows_t, 16, cuts * LANES), BF16),
             pltpu.VMEM((dp, 2, own_q // 2, 16, cuts * LANES), BF16),
             pltpu.VMEM((2, 2, mods * 2 * width, 4 * width), BF16),
@@ -219,16 +295,17 @@
             pltpu.VMEM((rows_t, own_q * 16), F32),
             pltpu.VMEM((nmod, own_q, rows_t), F32),
             pltpu.VMEM((nmod, own_q, rows_t), F32),
+            pltpu.SemaphoreType.DMA((4,)),
             pltpu.SemaphoreType.DMA((cuts,)),
-            pltpu.SemaphoreType.DMA((dp,)),
-            pltpu.SemaphoreType.DMA((dp,)),
-            pltpu.SemaphoreType.DMA((dp,)),
-            pltpu.SemaphoreType.DMA((dp,)),
+            pltpu.SemaphoreType.DMA((2, dp, half_q)),
+            pltpu.SemaphoreType.DMA((dp, half_q)),
+            pltpu.SemaphoreType.DMA((dp, half_q)),
+            pltpu.SemaphoreType.DMA((dp, half_q)),
             pltpu.SemaphoreType.DMA((nmod,)),
             pltpu.SemaphoreType.DMA((nmod,)),
         ],
         compiler_params=pltpu.CompilerParams(
-            collective_id=0, has_side_effects=True, vmem_limit_bytes=40 * 1024 * 1024),
+            collective_id=0, has_side_effects=True, vmem_limit_bytes=60 * 1024 * 1024),
     )(by_tile(queries), batch, inv_out, inv_in, by_tile(train_store), jnp.transpose(row_scale))
 
 

time: 36.2 us -> 26 us (0.72)
  the two profiles are of different devices: /device:TPU:1 before, /device:TPU:0 now
where the time goes in v2:
time: 26 us; the launch traced here: 25.8 us
  Pallas kernels  24.5 us (94%)
  local copies, waits for them, and re-layouts  1.28 us (5%)
    pallas_call x1, Pallas kernels, shards(): pl.pallas_call(functools.partial(kernel, sizes), out_shape=jax.ShapeDtype...  24.5 us
    unnamed x1, local copies, waits for them, and re-layouts  1.28 us

profile of v2, /device:TPU:0, one launch (start us, length us, event | category | flops | bytes accessed | tf_op | source)
XLA Modules:
  0.0 25.8 jit_solution(10296513059941880244)
XLA Ops:
  0.0 24.5 %shard_map.64 = f32[8,128]{1,0:T(8,128)} custom-call(bf16[8,128,128]{2,1,0:T(8,128)(2,1)} %bitcast.12, s32[8]{0:T(128)} %batch_ref.1, f32[2,4,64,64]{3,2,1,0:T(8,128)} %out_hbm.1, f32[2,4,64,64]{3,2,1,0:T(8,128)} %in_hbm.1, bf16[128,128,128]{2,1,0:T(8,128)(2,1)} %bitcast.11, f32[4,128]{1,0:T(4,128)} %bitcast.13), custom_call_target="tpu_custom_call" | custom-call | tf_op jit(solution)/shard_map/pallas_call | solution.py:281
  24.6 1.3 %copy.10 = f32[8,128]{1,0:T(8,128)} copy(f32[8,128]{1,0:T(8,128)} %shard_map.64) | data formatting | bytes 8192

commit v3 on v2

--- a/solution.py
+++ b/solution.py
@@ -171,6 +171,49 @@
             def _():
                 z_copy(z, i, way).start()
 
+    def score(origin):
+        pre = preb[origin].reshape(cols, cuts * LANES)
+        raw = mat_t(tcat[...].reshape(rows_t * group, cuts * LANES), pre).reshape(rows_t, group, cols)
+        keep = iota((rows_t, group, cols), 1) == iota((rows_t, group, cols), 2) % group
+        picked = jnp.sum(jnp.where(keep, raw, 0.0), axis=1) * scale_x[...]
+        part[origin] = sum(mat_t(fold, p) for p in three(picked))
+
+        @pl.when(origin != md)
+        def _():
+            m_copy(origin, md).start()
+
+    def source(d, way):
+        origin = z - d if way == 0 else z + d
+        return jnp.clip(origin, 0, dp - 1), (origin >= 0) & (origin < dp)
+
+    def pass_on(d, i):
+        for way in range(2):
+            origin, there = source(d, way)
+
+            @pl.when(there)
+            def _():
+                z_copy(origin, i, way).wait_recv()
+
+                @pl.when(has_next(way))
+                def _():
+                    z_copy(origin, i, way).start()
+
+                y_copy(origin, y, i).start()
+
+    def use(d):
+        for way in range(2):
+            origin, there = source(d, way)
+
+            @pl.when(there)
+            def _():
+                for i in range(half_q):
+                    y_copy(origin, other, i).wait_recv()
+                score(origin)
+
+    for i in range(half_q):
+        pass_on(1, i)
+        precondition(other * half_q + i, other, i)
+
     locals_in[3].wait()
     pick_mod = ones_where(iota((mods, cols), 0) == iota((mods, cols), 1) % mods)
     scale_x[...] = sum(
@@ -181,48 +224,6 @@
     for g in range(cuts):
         train_copy(g).wait()
 
-    def score(origin):
-        pre = preb[origin].reshape(cols, cuts * LANES)
-        raw = mat_t(tcat[...].reshape(rows_t * group, cuts * LANES), pre).reshape(rows_t, group, cols)
-        keep = iota((rows_t, group, cols), 1) == iota((rows_t, group, cols), 2) % group
-        picked = jnp.sum(jnp.where(keep, raw, 0.0), axis=1) * scale_x[...]
-        part[origin] = sum(mat_t(fold, p) for p in three(picked))
-
-        @pl.when(origin != md)
-        def _():
-            m_copy(origin, md).start()
-
-    def source(d, way):
-        origin = z - d if way == 0 else z + d
-        return jnp.clip(origin, 0, dp - 1), (origin >= 0) & (origin < dp)
-
-    def pass_on(d, i):
-        for way in range(2):
-            origin, there = source(d, way)
-
-            @pl.when(there)
-            def _():
-                z_copy(origin, i, way).wait_recv()
-
-                @pl.when(has_next(way))
-                def _():
-                    z_copy(origin, i, way).start()
-
-                y_copy(origin, y, i).start()
-
-    def use(d):
-        for way in range(2):
-            origin, there = source(d, way)
-
-            @pl.when(there)
-            def _():
-                for i in range(half_q):
-                    y_copy(origin, other, i).wait_recv()
-                score(origin)
-
-    for i in range(half_q):
-        pass_on(1, i)
-        precondition(other * half_q + i, other, i)
     score(z)
 
     def step(d, carry):

time: 26 us -> 26 us (level)
  no operation moved by 1% of the time
where the time goes in v3:
time: 26 us; the launch traced here: 25.8 us
  Pallas kernels  24.5 us (94%)
  local copies, waits for them, and re-layouts  1.28 us (5%)
    pallas_call x1, Pallas kernels, shards(): pl.pallas_call(functools.partial(kernel, sizes), out_shape=jax.ShapeDtype...  24.5 us
    unnamed x1, local copies, waits for them, and re-layouts  1.28 us

profile of v3, /device:TPU:0, one launch (start us, length us, event | category | flops | bytes accessed | tf_op | source)
XLA Modules:
  0.0 25.8 jit_solution(3144204534351909015)
XLA Ops:
  0.0 24.5 %shard_map.64 = f32[8,128]{1,0:T(8,128)} custom-call(bf16[8,128,128]{2,1,0:T(8,128)(2,1)} %bitcast.12, s32[8]{0:T(128)} %batch_ref.1, f32[2,4,64,64]{3,2,1,0:T(8,128)} %out_hbm.1, f32[2,4,64,64]{3,2,1,0:T(8,128)} %in_hbm.1, bf16[128,128,128]{2,1,0:T(8,128)(2,1)} %bitcast.11, f32[4,128]{1,0:T(4,128)} %bitcast.13), custom_call_target="tpu_custom_call" | custom-call | tf_op jit(solution)/shard_map/pallas_call | solution.py:282
  24.6 1.3 %copy.10 = f32[8,128]{1,0:T(8,128)} copy(f32[8,128]{1,0:T(8,128)} %shard_map.64) | data formatting | bytes 8192
